TPU v7x, 128 devices: a whole 4x4x4 slice. The times are simulated.
128 devices in a mesh: spec: 16 (over y_lo, x, core), wave: 8 (over z, y_hi).
Axes of the slice: x: 4, y: 4 (y_hi: 2, y_lo: 2; y = y_hi * 2 + y_lo), z: 4, core: 2. Of those that a mesh axis runs over, the one named last changes fastest.
Arguments:
- spectra: bfloat16 [16384, 7168], P('spec', 'wave'), may hold values from 0.049804688 to 5
- offsets: int32 [64], P('spec'), may hold values from 0 to 7167, as said below
- cover_lo: int32 [16384], P('spec'), may hold values from 0 to 7167, as said below
- cover_hi: int32 [16384], P('spec'), may hold values from 5377 to 7168
- coefficients: float32 [16384, 128], P('spec'), may hold values from 0.03 to 0.3
- templates: float32 [128, 7168], P(None, 'wave'), may hold values from 0.03 to 0.3
Outputs:
- templates_new: float32 [128, 7168], P(None, 'wave')
- coefficients_new: float32 [16384, 128], P('spec')
Inputs may be any that keep to these rules, and one draw needn't show every extreme that they name: `offsets`: the first block of each index of spec has an offset of at least 6272; the last block's offset is 7167. cover_lo < cover_hi for every spectrum; about one spectrum in eight has weight one only on its last 1 to 4 observed pixels, cover_hi = 7168; the others have cover_lo < 1792 and cover_hi > 5376.
All inputs are finite; a program needn't handle non-finite values.
Results may differ from a plain program's by a relative error of at most 0.0012.
Values may be sent and summed in bfloat16 or wider, within the bound.
No kernel may reach another device: no remote copies, remote signals or barrier semaphores. Data moves between devices by JAX's collectives and lax.ppermute only.
A program may use at most 128 MiB of HBM per device.

v0:
```python
import jax
import jax.numpy as jnp
from jax import lax
from jax.sharding import PartitionSpec as P

ITERS = 4


def take_blocks(joined, starts, blocks, width):
    rows = joined.shape[0]
    grouped = joined.reshape(blocks, rows // blocks, joined.shape[1])
    picked = jax.vmap(lambda piece, start: lax.dynamic_slice_in_dim(piece, start, width, 1))(
        grouped, starts
    )
    return picked.reshape(rows, width)


def ratio_of(rest, weight, coef_bf, temps_bf):
    model = jnp.dot(coef_bf, temps_bf, preferred_element_type=jnp.float32)
    inside = weight > 0
    return jnp.where(inside, rest.astype(jnp.float32) / jnp.where(inside, model, 1.0), 0.0).astype(
        jnp.bfloat16
    )


def over_rows(left, right):
    return lax.dot_general(
        left, right, (((0,), (0,)), ((), ())), preferred_element_type=jnp.float32
    )


def over_pixels(left, right):
    return lax.dot_general(
        left, right, (((1,), (1,)), ((), ())), preferred_element_type=jnp.float32
    )


def template_update(temps, num_t, den_t):
    num_a, den_a = lax.psum((num_t, den_t), "spec")
    return temps * num_a / jnp.maximum(den_a, 1.0)


def coef_update(coef, num_c, den_c):
    num_a, den_a = lax.psum((num_c, den_c), "wave")
    return coef * num_a / jnp.maximum(den_a, 1.0)


def shards(spectra, offsets, cover_lo, cover_hi, coefficients, templates):
    rows, width = spectra.shape
    blocks = offsets.shape[0]
    block_rows = rows // blocks
    wave_pos = lax.axis_index("wave")
    row_off = jnp.repeat(offsets, block_rows)
    whole = lax.all_gather(spectra, "wave", axis=1, tiled=True)
    joined = jnp.concatenate([whole, jnp.zeros((rows, width), whole.dtype)], axis=1)
    starts = jnp.minimum(wave_pos * width + offsets, whole.shape[1])
    rest = take_blocks(joined, starts, blocks, width)
    pixel = wave_pos * width + jnp.arange(width, dtype=jnp.int32)
    observed = pixel[None, :] + row_off[:, None]
    weight = ((observed >= cover_lo[:, None]) & (observed < cover_hi[:, None])).astype(jnp.bfloat16)
    temps = templates
    coef = coefficients
    for update in range(ITERS):
        coef_bf = coef.astype(jnp.bfloat16)
        ratio = ratio_of(rest, weight, coef_bf, temps.astype(jnp.bfloat16))
        temps = template_update(temps, over_rows(coef_bf, ratio), over_rows(coef_bf, weight))
        temps_bf = temps.astype(jnp.bfloat16)
        ratio_new = ratio_of(rest, weight, coef_bf, temps_bf)
        coef = coef_update(coef, over_pixels(ratio_new, temps_bf), over_pixels(weight, temps_bf))
    return (temps, coef)


def solution(mesh):
    in_specs = (
        P("spec", "wave"),
        P("spec"),
        P("spec"),
        P("spec"),
        P("spec", None),
        P(None, "wave"),
    )
    out_specs = (P(None, "wave"), P("spec", None))
    return jax.shard_map(shards, mesh=mesh, in_specs=in_specs, out_specs=out_specs, check_vma=False)
```

profile of v0, /device:TPU:0, one launch (start us, length us, event | category | flops | bytes accessed | tf_op | source)
XLA Modules:
  0.0 1094.5 jit_solution(7808599163899580070)
XLA Ops:
  7.2 0.0 all-gather.2.cloned.1.call-start
  7.2 0.7 all-gather.2.cloned.1.call-update
  7.9 0.0 all-reduce.25.cloned.1.call-start
  8.0 0.7 broadcast_bitcast_fusion
  8.7 0.7 fusion.32
  9.4 0.1 copy.8
  9.5 3.4 convolution_bitcast_fusion
  12.9 163.0 %all-gather.2.cloned.1.call-done = bf16[1024,7168]{1,0:T(8,128)(2,1)} async-done(((bf16[1024,896]{1,0:T(8,128)(2,1)}), bf16[1024,7168]{1,0:T(8,128)(2,1)}) %all-gather.2.cloned.1.call-update) | async-done | bytes 14680080 | tf_op jit(solution)/shard_map/all_gather | solution.py:54
  175.9 12.9 %concatenate.6 = bf16[1024,8064]{1,0:T(8,128)(2,1)} pad(bf16[1024,7168]{1,0:T(8,128)(2,1)} %all-gather.2.cloned.1.call-done, bf16[]{:T(256)} %constant.10.clone.1), padding=0_0x0_896 | pad | bytes 31195138 | tf_op jit(solution)/shard_map/concatenate | solution.py:55
  188.8 12.5 %while.1 = (s32[]{:T(128)}, bf16[4,256,8064]{2,1,0:T(8,128)(2,1)}, s32[4,3]{1,0:T(4,128)S(1)}, bf16[4,256,896]{2,1,0:T(8,128)(2,1)S(1)}, s32[]{:T(128)}) while((s32[]{:T(128)}, bf16[4,256,8064]{2,1,0:T(8,128)(2,1)}, s32[4,3]{1,0:T(4,128)S(1)}, bf16[4,256,896]{2,1,0:T(8,128)(2,1)S(1)}, s32[]{:T(128)}) %tuple.54), condition=%wide.while_cond, body=%wide.while_body.sunk | while | flops 2 | bytes 917621 | solution.py:12
  188.8 0.6 fusion.108
  189.4 2.5 dynamic-slice_dynamic-update-slice_fusion.2
  191.9 0.6 fusion.108
  192.5 2.5 dynamic-slice_dynamic-update-slice_fusion.2
  195.1 0.6 fusion.108
  195.7 2.5 dynamic-slice_dynamic-update-slice_fusion.2
  198.2 0.6 fusion.108
  198.8 2.5 dynamic-slice_dynamic-update-slice_fusion.2
  201.4 2.9 fusion.25
  204.3 0.0 all-reduce.25.cloned.1.call-update
  204.3 0.0 all-reduce.33.cloned.1.call-start
  204.3 0.2 copy.9
  204.5 116.8 %all-reduce.25.cloned.1.call-done = (f32[128,896]{0,1:T(8,128)}, f32[128,896]{0,1:T(8,128)}) async-done(((f32[128,896]{0,1:T(8,128)}, f32[128,896]{0,1:T(8,128)}), (f32[128,896]{0,1:T(8,128)}, f32[128,896]{0,1:T(8,128)})) %all-reduce.25.cloned.1.call-update) | async-done | bytes 917520 | tf_op jit(solution)/shard_map/psum | solution.py:39
  321.3 1.2 maximum_divide_fusion.7
  322.6 2.5 fusion.20
  325.1 2.0 fusion.63
  327.0 0.0 all-reduce.33.cloned.1.call-update
  327.1 0.0 all-reduce.23.cloned.1.call-start
  327.1 92.3 %all-reduce.33.cloned.1.call-done = (f32[1024,128]{1,0:T(8,128)}, f32[1024,128]{1,0:T(8,128)}) async-done(((f32[1024,128]{1,0:T(8,128)}, f32[1024,128]{1,0:T(8,128)}), (f32[1024,128]{1,0:T(8,128)}, f32[1024,128]{1,0:T(8,128)})) %all-reduce.33.cloned.1.call-update) | async-done | bytes 1048592 | tf_op jit(solution)/shard_map/psum | solution.py:44
  419.4 1.3 maximum_divide_fusion.3
  420.7 3.2 fusion.24
  423.9 2.4 fusion.57
  426.3 0.0 all-reduce.23.cloned.1.call-update
  426.3 0.2 all-reduce.31.cloned.1.call-start
  426.5 117.0 %all-reduce.23.cloned.1.call-done = (f32[128,896]{0,1:T(8,128)}, f32[128,896]{0,1:T(8,128)}) async-done(((f32[128,896]{0,1:T(8,128)}, f32[128,896]{0,1:T(8,128)}), (f32[128,896]{0,1:T(8,128)}, f32[128,896]{0,1:T(8,128)})) %all-reduce.23.cloned.1.call-update) | async-done | bytes 917520 | tf_op jit(solution)/shard_map/psum | solution.py:39
  543.5 1.2 maximum_divide_fusion.6
  544.7 2.5 fusion.19
  547.3 2.0 fusion.51
  549.2 0.0 all-reduce.21.cloned.1.call-start
  549.3 92.2 %all-reduce.31.cloned.1.call-done = (f32[1024,128]{1,0:T(8,128)}, f32[1024,128]{1,0:T(8,128)}) async-done(((f32[1024,128]{1,0:T(8,128)}, f32[1024,128]{1,0:T(8,128)}), (f32[1024,128]{1,0:T(8,128)}, f32[1024,128]{1,0:T(8,128)})) %all-reduce.31.cloned.1.call-update) | async-done | bytes 1048592 | tf_op jit(solution)/shard_map/psum | solution.py:44
  641.5 1.3 maximum_divide_fusion.2
  642.8 3.2 fusion.23
  646.0 2.4 fusion.45
  648.4 0.0 all-reduce.21.cloned.1.call-update
  648.4 0.0 all-reduce.29.cloned.1.call-start
  648.5 117.2 %all-reduce.21.cloned.1.call-done = (f32[128,896]{0,1:T(8,128)}, f32[128,896]{0,1:T(8,128)}) async-done(((f32[128,896]{0,1:T(8,128)}, f32[128,896]{0,1:T(8,128)}), (f32[128,896]{0,1:T(8,128)}, f32[128,896]{0,1:T(8,128)})) %all-reduce.21.cloned.1.call-update) | async-done | bytes 917520 | tf_op jit(solution)/shard_map/psum | solution.py:39
  765.6 1.2 maximum_divide_fusion.5
  766.8 2.5 fusion.18
  769.4 2.0 fusion.39
  771.3 0.0 all-reduce.29.cloned.1.call-update
  771.4 0.3 all-reduce.19.cloned.1.call-start
  771.6 92.1 %all-reduce.29.cloned.1.call-done = (f32[1024,128]{1,0:T(8,128)}, f32[1024,128]{1,0:T(8,128)}) async-done(((f32[1024,128]{1,0:T(8,128)}, f32[1024,128]{1,0:T(8,128)}), (f32[1024,128]{1,0:T(8,128)}, f32[1024,128]{1,0:T(8,128)})) %all-reduce.29.cloned.1.call-update) | async-done | bytes 1048592 | tf_op jit(solution)/shard_map/psum | solution.py:44
  863.7 1.3 maximum_divide_fusion.1
  865.0 3.2 fusion.22
  868.2 2.4 fusion.33
  870.5 0.0 all-reduce.19.cloned.1.call-update
  870.6 0.0 all-reduce.27.cloned.1.call-start
  870.6 117.2 %all-reduce.19.cloned.1.call-done = (f32[128,896]{0,1:T(8,128)}, f32[128,896]{0,1:T(8,128)}) async-done(((f32[128,896]{0,1:T(8,128)}, f32[128,896]{0,1:T(8,128)}), (f32[128,896]{0,1:T(8,128)}, f32[128,896]{0,1:T(8,128)})) %all-reduce.19.cloned.1.call-update) | async-done | bytes 917520 | tf_op jit(solution)/shard_map/psum | solution.py:39
  987.8 1.2 maximum_divide_fusion.4
  989.0 2.5 fusion.17
  991.6 2.0 fusion.30
  993.5 1.0 copy.16
  994.5 91.4 %all-reduce.27.cloned.1.call-done = (f32[1024,128]{1,0:T(8,128)}, f32[1024,128]{1,0:T(8,128)}) async-done(((f32[1024,128]{1,0:T(8,128)}, f32[1024,128]{1,0:T(8,128)}), (f32[1024,128]{1,0:T(8,128)}, f32[1024,128]{1,0:T(8,128)})) %all-reduce.27.cloned.1.call-update) | async-done | bytes 1048592 | tf_op jit(solution)/shard_map/psum | solution.py:44
  1085.9 2.1 maximum_divide_fusion
  (19 shorter events, 0.1 us)
Async XLA Ops:
  7.2 168.7 %all-gather.2.cloned.1.call-start = ((), (), s32[]{:S(2)}) async-start(), calls=%async_computation | async-start | bytes 16515072 | tf_op jit(solution)/shard_map/all_gather | solution.py:54
  7.9 313.4 %all-reduce.25.cloned.1.call-start = ((), (), s32[]{:S(2)}) async-start(), calls=%async_computation.4 | async-start | bytes 1835008 | tf_op jit(solution)/shard_map/psum | solution.py:39
  175.9 25.5 %copy-start.1 = (f32[128,896]{1,0:T(8,128)S(1)}, f32[128,896]{1,0:T(8,128)}, u32[]{:S(2)}) copy-start(f32[128,896]{1,0:T(8,128)} %param.11) | copy-start | bytes 1376260
  188.8 12.6 %copy-start = (f32[1024,128]{1,0:T(8,128)S(1)}, f32[1024,128]{1,0:T(8,128)}, u32[]{:S(2)}) copy-start(f32[1024,128]{1,0:T(8,128)} %param.10) | copy-start | bytes 1572868
  188.8 12.6 %copy-start.2 = (s32[1024]{0:T(1024)S(1)}, s32[1024]{0:T(1024)}, u32[]{:S(2)}) copy-start(s32[1024]{0:T(1024)} %param.9) | copy-start | bytes 12292
  188.8 12.6 %copy-start.3 = (s32[1024]{0:T(1024)S(1)}, s32[1024]{0:T(1024)}, u32[]{:S(2)}) copy-start(s32[1024]{0:T(1024)} %param.8) | copy-start | bytes 12292
  204.3 215.1 %all-reduce.33.cloned.1.call-start = ((), (), s32[]{:S(2)}) async-start(), calls=%async_computation.8 | async-start | bytes 2097152 | tf_op jit(solution)/shard_map/psum | solution.py:44
  327.1 216.4 %all-reduce.23.cloned.1.call-start = ((), (), s32[]{:S(2)}) async-start(), calls=%async_computation.3 | async-start | bytes 1835008 | tf_op jit(solution)/shard_map/psum | solution.py:39
  426.3 215.2 %all-reduce.31.cloned.1.call-start = ((), (), s32[]{:S(2)}) async-start(), calls=%async_computation.7 | async-start | bytes 2097152 | tf_op jit(solution)/shard_map/psum | solution.py:44
  549.2 216.4 %all-reduce.21.cloned.1.call-start = ((), (), s32[]{:S(2)}) async-start(), calls=%async_computation.2 | async-start | bytes 1835008 | tf_op jit(solution)/shard_map/psum | solution.py:39
  648.4 215.3 %all-reduce.29.cloned.1.call-start = ((), (), s32[]{:S(2)}) async-start(), calls=%async_computation.6 | async-start | bytes 2097152 | tf_op jit(solution)/shard_map/psum | solution.py:44
  771.4 216.4 %all-reduce.19.cloned.1.call-start = ((), (), s32[]{:S(2)}) async-start(), calls=%async_computation.1 | async-start | bytes 1835008 | tf_op jit(solution)/shard_map/psum | solution.py:39
  870.6 215.3 %all-reduce.27.cloned.1.call-start = ((), (), s32[]{:S(2)}) async-start(), calls=%async_computation.5 | async-start | bytes 2097152 | tf_op jit(solution)/shard_map/psum | solution.py:44
Sparse Core Ops, SparseCore 0:
  10.4 165.4 all-gather.1
  204.4 116.8 all-reduce.24
  327.2 92.1 all-reduce.32
  426.4 117.0 all-reduce.22
  549.4 92.1 all-reduce.30
  648.5 117.0 all-reduce.20
  771.5 92.1 all-reduce.28
  870.7 117.0 all-reduce.18
  993.7 92.1 all-reduce.26
where the time goes:
time: 1100 us; the launch traced here: 1090 us
  waiting for transfers between devices  1000 us (91%)
  matrix products  41 us (4%)
  local copies, waits for them, and re-layouts  27.3 us (2%)
  between operations  13.9 us (1%)
  other arithmetic  11.5 us (1%)
    psum x4, waiting for transfers between devices, template_update(): num_a, den_a = lax.psum((num_t, den_t), 'spec')  468 us
    psum x4, waiting for transfers between devices, coef_update(): num_a, den_a = lax.psum((num_c, den_c), 'wave')  368 us
    all_gather x1, waiting for transfers between devices, shards(): whole = lax.all_gather(spectra, 'wave', axis=1, tiled=True)  163 us
    dot_general x8, matrix products, over_rows(): lax.dot_general(left, right, (((0,), (0,)), ((), ())), preferred_element_...  23.1 us
  transfers between devices with their start and end apart: 9, of which 9 were waited for; matrix products, arithmetic and copies ran while one was open for 1% of the time, Pallas kernels for 0%

commit v1 on v0

--- a/solution.py
+++ b/solution.py
@@ -51,7 +51,9 @@
     block_rows = rows // blocks
     wave_pos = lax.axis_index("wave")
     row_off = jnp.repeat(offsets, block_rows)
-    whole = lax.all_gather(spectra, "wave", axis=1, tiled=True)
+    whole = jnp.concatenate(
+        lax.all_to_all(jnp.stack([spectra] * lax.axis_size("wave")), "wave", 0, 0), axis=1
+    )
     joined = jnp.concatenate([whole, jnp.zeros((rows, width), whole.dtype)], axis=1)
     starts = jnp.minimum(wave_pos * width + offsets, whole.shape[1])
     rest = take_blocks(joined, starts, blocks, width)

time: 1100 us -> 1160 us (1.055)
  local copies, waits for them, and re-layouts: 27.3 us -> 75.4 us
    all_gather x1 -> x0, waiting for transfers between devices: 163 us -> none  [shards(): whole = lax.all_gather(spectra, 'wave', axis=1, tiled=True)]
    all_to_all x0 -> x1, waiting for transfers between devices: none -> 161 us  [shards(): lax.all_to_all(jnp.stack([spectra] * lax.axis_size('wave')), 'wave', 0, 0)]
    all_to_all x0 -> x1, local copies, waits for them, and re-layouts: none -> 20.7 us  [shards(): lax.all_to_all(jnp.stack([spectra] * lax.axis_size('wave')), 'wave', 0, 0)]
    unnamed x14 -> x17, local copies, waits for them, and re-layouts: 2 us -> 19.9 us
  transfers between devices with their start and end apart: 9 -> 9, of which waited for: 9 -> 9; matrix products, arithmetic and copies ran while one was open for 1% -> 0% of each run, Pallas kernels for 0% -> 0%
where the time goes in v1:
time: 1160 us
  waiting for transfers between devices  996 us (86%)
  local copies, waits for them, and re-layouts  75.4 us (7%)
  matrix products  51.2 us (4%)
  between operations  14.2 us (1%)
    psum x4, waiting for transfers between devices, template_update(): num_a, den_a = lax.psum((num_t, den_t), 'spec')  468 us
    psum x4, waiting for transfers between devices, coef_update(): num_a, den_a = lax.psum((num_c, den_c), 'wave')  368 us
    all_to_all x1, waiting for transfers between devices, shards(): lax.all_to_all(jnp.stack([spectra] * lax.axis_size('wave')), 'wave', 0, 0)  161 us
    dot_general x8, matrix products, over_rows(): lax.dot_general(left, right, (((0,), (0,)), ((), ())), preferred_element_...  27.5 us
    dot_general x8, matrix products, over_pixels(): lax.dot_general(left, right, (((1,), (1,)), ((), ())), preferred_element_...  23.7 us
  transfers between devices with their start and end apart: 9, of which 9 were waited for; matrix products, arithmetic and copies ran while one was open for 0% of the time, Pallas kernels for 0%

profile of v1, /device:TPU:0, one launch (start us, length us, event | category | flops | bytes accessed | tf_op | source)
XLA Modules:
  0.0 1156.9 jit_solution(5466918554296726977)
XLA Ops:
  7.2 6.5 stack.2
  13.7 8.2 all-to-all-start
  21.9 0.0 all-reduce.25.cloned.1.call-start
  21.9 0.1 broadcast_bitcast_fusion
  22.0 0.1 copy.28
  22.1 2.4 convolution_bitcast_fusion
  24.5 160.8 %all-to-all-done = bf16[8,1024,896]{2,1,0:T(8,128)(2,1)} async-done(((bf16[8,1024,896]{2,1,0:T(8,128)(2,1)}), bf16[8,1024,896]{2,1,0:T(8,128)(2,1)}, u32[]{:S(2)}, u32[]{:S(2)}) %all-to-all-start) | async-done | bytes 14680096 | tf_op jit(solution)/shard_map/all_to_all | solution.py:55
  185.3 20.7 %copy.26 = bf16[8,1024,896]{1,2,0:T(8,128)(2,1)} copy(bf16[8,1024,896]{2,1,0:T(8,128)(2,1)} %all-to-all-done) | data formatting | bytes 29360128 | tf_op jit(solution)/shard_map/all_to_all | solution.py:55
  205.9 18.5 %copy.46 = bf16[1024,7168]{1,0:T(8,128)(2,1)} copy(bf16[1024,7168]{0,1:T(8,128)(2,1)} %bitcast.27) | data formatting | bytes 29360128
  224.5 12.8 %concatenate.6.clone = bf16[1024,8064]{1,0:T(8,128)(2,1)} pad(bf16[1024,7168]{1,0:T(8,128)(2,1)} %copy.46, bf16[]{:T(256)} %constant.10.clone.1), padding=0_0x0_896 | pad | bytes 31195138 | tf_op jit(solution)/shard_map/concatenate | solution.py:57
  237.3 15.5 %while.1 = (s32[]{:T(128)}, bf16[4,256,8064]{2,1,0:T(8,128)(2,1)}, s32[4,3]{1,0:T(4,128)S(1)}, bf16[4,256,896]{2,1,0:T(8,128)(2,1)}, s32[]{:T(128)}) while((s32[]{:T(128)}, bf16[4,256,8064]{2,1,0:T(8,128)(2,1)}, s32[4,3]{1,0:T(4,128)S(1)}, bf16[4,256,896]{2,1,0:T(8,128)(2,1)}, s32[]{:T(128)}) %tuple.56), condition=%wide.while_cond, body=%wide.while_body.sunk | while | flops 2 | bytes 919145 | solution.py:12
  237.3 0.6 fusion.108
  237.9 3.3 dynamic-slice_dynamic-update-slice_fusion.2
  241.2 0.6 fusion.108
  241.8 3.3 dynamic-slice_dynamic-update-slice_fusion.2
  245.1 0.6 fusion.108
  245.7 3.3 dynamic-slice_dynamic-update-slice_fusion.2
  248.9 0.6 fusion.108
  249.5 3.3 dynamic-slice_dynamic-update-slice_fusion.2
  252.8 4.2 fusion.25
  257.1 0.0 all-reduce.33.cloned.1.call-start
  257.1 0.2 copy.29
  257.3 116.4 %all-reduce.25.cloned.1.call-done = (f32[128,896]{0,1:T(8,128)}, f32[128,896]{0,1:T(8,128)}) async-done(((f32[128,896]{0,1:T(8,128)}, f32[128,896]{0,1:T(8,128)}), (f32[128,896]{0,1:T(8,128)}, f32[128,896]{0,1:T(8,128)})) %all-reduce.25.cloned.1.call-update) | async-done | bytes 917520 | tf_op jit(solution)/shard_map/psum | solution.py:39
  373.7 1.2 maximum_divide_fusion.7
  374.9 4.0 fusion.20
  378.9 2.0 fusion.63
  380.8 0.0 all-reduce.33.cloned.1.call-update
  380.9 0.2 all-reduce.23.cloned.1.call-start
  381.1 92.0 %all-reduce.33.cloned.1.call-done = (f32[1024,128]{1,0:T(8,128)}, f32[1024,128]{1,0:T(8,128)}) async-done(((f32[1024,128]{1,0:T(8,128)}, f32[1024,128]{1,0:T(8,128)}), (f32[1024,128]{1,0:T(8,128)}, f32[1024,128]{1,0:T(8,128)})) %all-reduce.33.cloned.1.call-update) | async-done | bytes 1048592 | tf_op jit(solution)/shard_map/psum | solution.py:44
  473.1 1.3 maximum_divide_fusion.3
  474.4 4.6 fusion.24
  479.0 2.4 fusion.57
  481.4 0.0 all-reduce.23.cloned.1.call-update
  481.4 0.0 all-reduce.31.cloned.1.call-start
  481.4 117.2 %all-reduce.23.cloned.1.call-done = (f32[128,896]{0,1:T(8,128)}, f32[128,896]{0,1:T(8,128)}) async-done(((f32[128,896]{0,1:T(8,128)}, f32[128,896]{0,1:T(8,128)}), (f32[128,896]{0,1:T(8,128)}, f32[128,896]{0,1:T(8,128)})) %all-reduce.23.cloned.1.call-update) | async-done | bytes 917520 | tf_op jit(solution)/shard_map/psum | solution.py:39
  598.6 1.2 maximum_divide_fusion.6
  599.8 4.0 fusion.19
  603.8 2.0 fusion.51
  605.8 0.0 all-reduce.31.cloned.1.call-update
  605.8 0.0 all-reduce.21.cloned.1.call-start
  605.8 92.3 %all-reduce.31.cloned.1.call-done = (f32[1024,128]{1,0:T(8,128)}, f32[1024,128]{1,0:T(8,128)}) async-done(((f32[1024,128]{1,0:T(8,128)}, f32[1024,128]{1,0:T(8,128)}), (f32[1024,128]{1,0:T(8,128)}, f32[1024,128]{1,0:T(8,128)})) %all-reduce.31.cloned.1.call-update) | async-done | bytes 1048592 | tf_op jit(solution)/shard_map/psum | solution.py:44
  698.1 1.3 maximum_divide_fusion.2
  699.4 4.6 fusion.23
  704.0 2.4 fusion.45
  706.3 0.0 all-reduce.21.cloned.1.call-update
  706.4 0.3 all-reduce.29.cloned.1.call-start
  706.6 116.9 %all-reduce.21.cloned.1.call-done = (f32[128,896]{0,1:T(8,128)}, f32[128,896]{0,1:T(8,128)}) async-done(((f32[128,896]{0,1:T(8,128)}, f32[128,896]{0,1:T(8,128)}), (f32[128,896]{0,1:T(8,128)}, f32[128,896]{0,1:T(8,128)})) %all-reduce.21.cloned.1.call-update) | async-done | bytes 917520 | tf_op jit(solution)/shard_map/psum | solution.py:39
  823.6 1.2 maximum_divide_fusion.5
  824.8 4.0 fusion.18
  828.8 2.0 fusion.39
  830.7 0.0 all-reduce.29.cloned.1.call-update
  830.8 0.0 all-reduce.19.cloned.1.call-start
  830.8 92.2 %all-reduce.29.cloned.1.call-done = (f32[1024,128]{1,0:T(8,128)}, f32[1024,128]{1,0:T(8,128)}) async-done(((f32[1024,128]{1,0:T(8,128)}, f32[1024,128]{1,0:T(8,128)}), (f32[1024,128]{1,0:T(8,128)}, f32[1024,128]{1,0:T(8,128)})) %all-reduce.29.cloned.1.call-update) | async-done | bytes 1048592 | tf_op jit(solution)/shard_map/psum | solution.py:44
  923.0 1.3 maximum_divide_fusion.1
  924.3 4.6 fusion.22
  928.9 2.4 fusion.33
  931.3 0.0 all-reduce.27.cloned.1.call-start
  931.3 117.2 %all-reduce.19.cloned.1.call-done = (f32[128,896]{0,1:T(8,128)}, f32[128,896]{0,1:T(8,128)}) async-done(((f32[128,896]{0,1:T(8,128)}, f32[128,896]{0,1:T(8,128)}), (f32[128,896]{0,1:T(8,128)}, f32[128,896]{0,1:T(8,128)})) %all-reduce.19.cloned.1.call-update) | async-done | bytes 917520 | tf_op jit(solution)/shard_map/psum | solution.py:39
  1048.5 1.2 maximum_divide_fusion.4
  1049.7 4.0 fusion.17
  1053.7 2.0 fusion.30
  1055.7 1.0 copy.37
  1056.6 91.4 %all-reduce.27.cloned.1.call-done = (f32[1024,128]{1,0:T(8,128)}, f32[1024,128]{1,0:T(8,128)}) async-done(((f32[1024,128]{1,0:T(8,128)}, f32[1024,128]{1,0:T(8,128)}), (f32[1024,128]{1,0:T(8,128)}, f32[1024,128]{1,0:T(8,128)})) %all-reduce.27.cloned.1.call-update) | async-done | bytes 1048592 | tf_op jit(solution)/shard_map/psum | solution.py:44
  1148.0 2.1 maximum_divide_fusion
  (23 shorter events, 0.1 us)
Async XLA Ops:
  13.7 8.3 copy-start.2
  13.7 8.5 copy-start
  13.7 8.5 copy-start.3
  13.7 8.5 copy-start.4
  13.7 171.6 %all-to-all-start = ((bf16[8,1024,896]{2,1,0:T(8,128)(2,1)}), bf16[8,1024,896]{2,1,0:T(8,128)(2,1)}, u32[]{:S(2)}, u32[]{:S(2)}) async-start(bf16[8,1024,896]{2,1,0:T(8,128)(2,1)} %stack.2), calls=%async_computation | async-start | bytes 29360128 | tf_op jit(solution)/shard_map/all_to_all | solution.py:55
  21.9 351.8 %all-reduce.25.cloned.1.call-start = ((), (), s32[]{:S(2)}) async-start(), calls=%async_computation.4 | async-start | bytes 1835008 | tf_op jit(solution)/shard_map/psum | solution.py:39
  237.3 15.5 %copy-start.1 = (f32[128,896]{1,0:T(8,128)S(1)}, f32[128,896]{1,0:T(8,128)}, u32[]{:S(2)}) copy-start(f32[128,896]{1,0:T(8,128)} %param.11) | copy-start | bytes 1376260
  257.1 216.1 %all-reduce.33.cloned.1.call-start = ((), (), s32[]{:S(2)}) async-start(), calls=%async_computation.8 | async-start | bytes 2097152 | tf_op jit(solution)/shard_map/psum | solution.py:44
  380.9 217.7 %all-reduce.23.cloned.1.call-start = ((), (), s32[]{:S(2)}) async-start(), calls=%async_computation.3 | async-start | bytes 1835008 | tf_op jit(solution)/shard_map/psum | solution.py:39
  481.4 216.7 %all-reduce.31.cloned.1.call-start = ((), (), s32[]{:S(2)}) async-start(), calls=%async_computation.7 | async-start | bytes 2097152 | tf_op jit(solution)/shard_map/psum | solution.py:44
  605.8 217.8 %all-reduce.21.cloned.1.call-start = ((), (), s32[]{:S(2)}) async-start(), calls=%async_computation.2 | async-start | bytes 1835008 | tf_op jit(solution)/shard_map/psum | solution.py:39
  706.4 216.6 %all-reduce.29.cloned.1.call-start = ((), (), s32[]{:S(2)}) async-start(), calls=%async_computation.6 | async-start | bytes 2097152 | tf_op jit(solution)/shard_map/psum | solution.py:44
  830.8 217.7 %all-reduce.19.cloned.1.call-start = ((), (), s32[]{:S(2)}) async-start(), calls=%async_computation.1 | async-start | bytes 1835008 | tf_op jit(solution)/shard_map/psum | solution.py:39
  931.3 216.7 %all-reduce.27.cloned.1.call-start = ((), (), s32[]{:S(2)}) async-start(), calls=%async_computation.5 | async-start | bytes 2097152 | tf_op jit(solution)/shard_map/psum | solution.py:44
Sparse Core Ops, SparseCore 0:
  257.2 116.4 all-reduce.24
  381.0 92.0 all-reduce.32
  481.5 117.0 all-reduce.22
  605.9 92.1 all-reduce.30
  706.5 117.0 all-reduce.20
  830.9 92.0 all-reduce.28
  931.4 117.0 all-reduce.18
  1055.8 92.1 all-reduce.26
